TPU v7x, 32 devices: a whole 2x2x4 slice. The times are simulated.
32 devices in a mesh: groups: 2 (over y), replica: 4 (over z), tensor: 4 (over x, core).
Axes of the slice: x: 2, y: 2, z: 4, core: 2. Of those that a mesh axis runs over, the one named last changes fastest.
Arguments:
- hidden_input_saved: bfloat16 [4096, 5120], P(('groups', 'replica'), 'tensor'), parts along dimension 0, may hold values from -6 to 6
- value_output_gradient: bfloat16 [4096, 512], P(('groups', 'replica'), 'tensor'), parts along dimension 0, may hold values from -6 to 6
- frozen_value_weight: bfloat16 [5120, 512], P('tensor'), may hold values from -0.078125 to 0.078125
- adapter_lower_factor: bfloat16 [32, 16, 5120], P(('groups', 'replica'), None, 'tensor'), parts along dimension 0, may hold values from -0.078125 to 0.078125
- adapter_upper_factor: bfloat16 [32, 16, 512], P(('groups', 'replica'), None, 'tensor'), parts along dimension 0, may hold values from -1.5 to 1.5
- per_token_adapter: int32 [4096, 1], P(('groups', 'replica')), parts along dimension 0, may hold values from 0 to 15; in each aligned block of 512 rows (0 to 511, 512 to 1023, ...) at most 96 rows name the same one
- adapter_table_slot: int32 [32], P('groups'), parts along dimension 0, may hold values from 0 to 15, each once
Outputs:
- hidden_grad: bfloat16 [4096, 5120], P(('groups', 'replica'), 'tensor'), parts along dimension 0
- down_grad: bfloat16 [32, 16, 5120], P(('groups', 'replica'), None, 'tensor'), parts along dimension 0
- up_grad: bfloat16 [32, 16, 512], P(('groups', 'replica'), None, 'tensor'), parts along dimension 0
There are 2 independent parts, one for each index of `groups`. A program takes and returns all parts, laid end to end along the dimension named above; an argument that names none is the same for every part. Nothing has to cross between parts.
Inputs may be any that keep to these rules, and one draw needn't show every extreme that they name: `per_token_adapter`: every adapter is named by some token. Among the tokens of one index of replica at most 96 name the same adapter, a bound that some block reaches there. `adapter_table_slot`: each adapter has one slot; slot i is held by replica index i // 4.
All inputs are finite; a program needn't handle non-finite values.
Results may differ from a plain program's by a relative error of at most 0.0055.
Values may be sent and summed in bfloat16 or wider, within the bound.
A program may use at most 64 MiB of HBM per device.

v0:
```python
import jax
import jax.numpy as jnp
from jax import lax
from jax.sharding import PartitionSpec as P

SCALING = 2.0


def shards(
    hidden_input_saved,
    value_output_gradient,
    frozen_value_weight,
    adapter_lower_factor,
    adapter_upper_factor,
    per_token_adapter,
    adapter_table_slot,
):
    replicas = lax.axis_size("replica")
    local_owned_count, reduced_rank_product, share_width = adapter_lower_factor.shape
    value_head_share = adapter_upper_factor.shape[2]
    tokens_here = hidden_input_saved.shape[0]
    adapters = local_owned_count * replicas
    capacity = max(2, 3 * tokens_here // adapters)
    slot_total_count = adapters * capacity
    full_grad = lax.all_gather(value_output_gradient, "tensor", axis=1, tiled=True)
    base_grad = lax.dot_general(
        full_grad, frozen_value_weight, (((1,), (1,)), ((), ())), preferred_element_type=jnp.float32
    )
    adapter_ids = per_token_adapter[:, 0]
    catalog = jnp.arange(adapters, dtype=jnp.int32)
    slot_ids = jnp.sum(
        jnp.where(adapter_ids[:, None] == catalog[None, :], adapter_table_slot[None, :], 0), axis=1
    )
    one_hot = (slot_ids[:, None] == catalog[None, :]).astype(jnp.int32)
    position = jnp.sum(one_hot * jnp.cumsum(one_hot, axis=0), axis=1) - 1
    destination_index = slot_ids * capacity + position
    rows_send = (
        jnp.zeros((slot_total_count, share_width), jnp.bfloat16)
        .at[destination_index]
        .set(hidden_input_saved)
    )
    value_send = (
        jnp.zeros((slot_total_count, value_head_share), jnp.bfloat16)
        .at[destination_index]
        .set(value_output_gradient)
    )
    marks_send = (
        jnp.zeros((slot_total_count,), jnp.bfloat16)
        .at[destination_index]
        .set(jnp.ones((tokens_here,), jnp.bfloat16))
    )
    incoming_rows, value_input_rows, marks_in = (
        lax.all_to_all(
            rows_send.reshape(replicas, local_owned_count, capacity, share_width),
            "replica",
            split_axis=0,
            concat_axis=0,
            tiled=True,
        ),
        lax.all_to_all(
            value_send.reshape(replicas, local_owned_count, capacity, value_head_share),
            "replica",
            split_axis=0,
            concat_axis=0,
            tiled=True,
        ),
        lax.all_to_all(
            marks_send.reshape(replicas, local_owned_count, capacity),
            "replica",
            split_axis=0,
            concat_axis=0,
            tiled=True,
        ),
    )
    lower_factor_share = jnp.einsum(
        "woip,osp->oswi", incoming_rows, adapter_lower_factor, preferred_element_type=jnp.float32
    )
    upper_factor_share = jnp.einsum(
        "xluq,liq->lixu", value_input_rows, adapter_upper_factor, preferred_element_type=jnp.float32
    )
    flat_shape = (local_owned_count, reduced_rank_product, replicas * capacity)
    down_sum, up_sum = lax.psum(
        (lower_factor_share.reshape(flat_shape), upper_factor_share.reshape(flat_shape)), "tensor"
    )
    coeff_down = down_sum.reshape(lower_factor_share.shape).astype(jnp.bfloat16)
    upper_coefficient = up_sum.reshape(upper_factor_share.shape).astype(jnp.bfloat16)
    counts = jnp.sum(marks_in.astype(jnp.float32), axis=(0, 2))
    factor = SCALING / counts
    down_grad = (
        jnp.einsum(
            "arnc,nacd->ard", upper_coefficient, incoming_rows, preferred_element_type=jnp.float32
        )
        * factor[:, None, None]
    ).astype(jnp.bfloat16)
    up_grad = (
        jnp.einsum(
            "arnc,nace->are", coeff_down, value_input_rows, preferred_element_type=jnp.float32
        )
        * factor[:, None, None]
    ).astype(jnp.bfloat16)
    coeff_send = jnp.transpose(upper_coefficient, (2, 0, 3, 1))
    coeff_back = lax.all_to_all(
        coeff_send, "replica", split_axis=0, concat_axis=0, tiled=True
    ).reshape(adapters, capacity, reduced_rank_product)
    adapter_token_rows = (
        jnp.einsum(
            "acr,ard->acd",
            coeff_back,
            lax.all_gather(adapter_lower_factor, "replica", axis=0, tiled=True),
            preferred_element_type=jnp.float32,
        )
        .astype(jnp.bfloat16)
        .reshape(slot_total_count, share_width)
    )
    selected_rows = adapter_token_rows[destination_index]
    hidden_grad = (base_grad + SCALING * selected_rows.astype(jnp.float32)).astype(jnp.bfloat16)
    return (hidden_grad, down_grad, up_grad)


def solution(mesh):
    placed = (
        P(("groups", "replica"), "tensor"),
        P(("groups", "replica"), "tensor"),
        P("tensor", None),
        P(("groups", "replica"), None, "tensor"),
        P(("groups", "replica"), None, "tensor"),
        P(("groups", "replica"), None),
        P("groups"),
    )
    return jax.shard_map(
        shards,
        mesh=mesh,
        in_specs=placed,
        out_specs=(
            P(("groups", "replica"), "tensor"),
            P(("groups", "replica"), None, "tensor"),
            P(("groups", "replica"), None, "tensor"),
        ),
        check_vma=False,
    )
```

profile of v0, /device:TPU:0, one launch (start us, length us, event | category | flops | bytes accessed | tf_op | source)
XLA Modules:
  0.0 174.0 jit_solution(6956182110587793193)
XLA Ops:
  0.6 0.0 copy-start
  0.6 0.9 select_reduce_fusion
  1.5 1.1 reduce-window.6
  2.7 0.2 slice_reduce_fusion
  3.0 0.1 fusion.29
  3.1 3.8 %scatter_custom_fusion.2 = bf16[1536]{0:T(1024)(128)(2,1)S(1)} fusion(s32[512]{0:T(512)S(1)} %bitcast.61, bf16[512]{0:T(512)(128)(2,1)S(1)} %broadcast.67, bf16[]{:T(256)} %constant.8.clone.1), kind=kCustom, calls=%fused_computation.42 | custom fusion | bytes 3074 | tf_op jit(solution)/shard_map/scatter | solution.py:50
  6.9 0.7 reshape.88
  7.6 6.3 %all-to-all-start.3 = ((bf16[4,4,96]{2,1,0:T(4,128)(2,1)}), bf16[4,4,96]{2,1,0:T(4,128)(2,1)S(1)}, u32[]{:S(2)}, u32[]{:S(2)}) async-start(bf16[4,4,96]{2,1,0:T(4,128)(2,1)} %reshape.88), calls=%async_computation.3 | async-start | bytes 8192 | tf_op jit(solution)/shard_map/all_to_all | solution.py:67
  13.9 2.9 %scatter_custom_fusion = bf16[1536,128]{1,0:T(8,128)(2,1)} fusion(s32[512]{0:T(512)S(1)} %bitcast.62, bf16[512,128]{1,0:T(8,128)(2,1)} %param.8, bf16[]{:T(256)} %constant.8.clone.1), kind=kCustom, calls=%fused_computation.23 | custom fusion | bytes 393728 | tf_op jit(solution)/shard_map/scatter | solution.py:45
  16.7 2.7 %all-to-all-done.3 = bf16[4,4,96]{2,1,0:T(4,128)(2,1)S(1)} async-done(((bf16[4,4,96]{2,1,0:T(4,128)(2,1)}), bf16[4,4,96]{2,1,0:T(4,128)(2,1)S(1)}, u32[]{:S(2)}, u32[]{:S(2)}) %all-to-all-start.3) | async-done | bytes 3104 | tf_op jit(solution)/shard_map/all_to_all | solution.py:67
  19.4 3.5 %all-to-all-start = ((bf16[4,4,96,128]{3,2,1,0:T(8,128)(2,1)}), bf16[4,4,96,128]{3,2,1,0:T(8,128)(2,1)S(1)}, u32[]{:S(2)}, u32[]{:S(2)}) async-start(bf16[4,4,96,128]{3,2,1,0:T(8,128)(2,1)} %bitcast.5), calls=%async_computation | async-start | bytes 786432 | tf_op jit(solution)/shard_map/all_to_all | solution.py:60
  22.9 6.1 %scatter_custom_fusion.1 = bf16[1536,1280]{1,0:T(8,128)(2,1)} fusion(s32[512]{0:T(512)S(1)} %bitcast.63, bf16[512,1280]{1,0:T(8,128)(2,1)} %param.7, bf16[]{:T(256)} %constant.8.clone.1), kind=kCustom, calls=%fused_computation.14 | custom fusion | bytes 3932672 | tf_op jit(solution)/shard_map/scatter | solution.py:40
  29.0 4.4 %all-to-all-done = bf16[4,4,96,128]{3,2,1,0:T(8,128)(2,1)S(1)} async-done(((bf16[4,4,96,128]{3,2,1,0:T(8,128)(2,1)}), bf16[4,4,96,128]{3,2,1,0:T(8,128)(2,1)S(1)}, u32[]{:S(2)}, u32[]{:S(2)}) %all-to-all-start) | async-done | bytes 393248 | tf_op jit(solution)/shard_map/all_to_all | solution.py:60
  33.4 0.0 copy-start.2
  33.4 0.0 copy-start.1
  33.4 0.0 copy-start.3
  33.4 4.9 %all-to-all-start.2 = ((bf16[4,4,96,1280]{3,2,1,0:T(8,128)(2,1)}), bf16[4,4,96,1280]{3,2,1,0:T(8,128)(2,1)}, u32[]{:S(2)}, u32[]{:S(2)}) async-start(bf16[4,4,96,1280]{3,2,1,0:T(8,128)(2,1)} %bitcast.57), calls=%async_computation.2 | async-start | bytes 7864320 | tf_op jit(solution)/shard_map/all_to_all | solution.py:53
  38.4 0.0 copy-done.2
  38.4 7.2 %all_gather.6 = bf16[512,512]{1,0:T(8,128)(2,1)S(1)} all-gather(bf16[512,128]{1,0:T(8,128)(2,1)S(1)} %copy-done.2), channel_id=1, replica_groups=mesh['groups'=2,'replica'=4,'tensor'=4] {'tensor'}, dimensions={1}, use_global_device_ids=true | all-gather | bytes 655360 | tf_op jit(solution)/shard_map/all_gather | solution.py:25
  45.6 0.0 copy-done.1
  45.6 89.5 %all_gather.7 = bf16[16,16,1280]{2,1,0:T(8,128)(2,1)S(1)} all-gather(bf16[4,16,1280]{2,1,0:T(8,128)(2,1)S(1)} %copy-done.1), channel_id=1, replica_groups=mesh['groups'=2,'replica'=4,'tensor'=4] {'replica'}, dimensions={0}, use_global_device_ids=true | all-gather | bytes 819200 | tf_op jit(solution)/shard_map/all_gather | solution.py:109
  135.1 0.1 convert_reduce_fusion
  135.2 0.0 copy-done.3
  135.2 0.3 convolution_bitcast_fusion
  135.6 0.1 copy.31
  135.6 0.1 reshape.84
  135.8 0.0 all-to-all-done.2
  135.8 3.4 %fusion.16 = f32[4,16,4,96]{3,1,2,0:T(8,128)S(1)} fusion(bf16[4,4,96,1280]{3,2,1,0:T(8,128)(2,1)} %all-to-all-done.2, bf16[4,16,1280]{2,1,0:T(8,128)(2,1)S(1)} %copy-done.1), kind=kOutput, calls=%fused_computation.17 | convolution fusion | flops 62914560 | bytes 4194304 | tf_op jit(solution)/shard_map/woip,osp->oswi/dot_general | solution.py:75
  139.2 0.1 copy.36
  139.2 0.1 reshape.89
  139.4 12.2 %all-reduce.2 = (bf16[4,16,384]{2,1,0:T(8,128)(2,1)S(1)}, bf16[4,16,384]{2,1,0:T(8,128)(2,1)S(1)}) all-reduce(f32[4,16,384]{2,1,0:T(8,128)S(1)} %reshape.84, f32[4,16,384]{2,1,0:T(8,128)S(1)} %reshape.89), channel_id=1, replica_groups=mesh['groups'=2,'replica'=4,'tensor'=4] {'tensor'}, use_global_device_ids=true, to_apply=%region_5.6 | all-reduce | flops 49152 | bytes 294912 | tf_op jit(solution)/shard_map/psum | solution.py:82
  151.5 0.1 convert_element_type.37
  151.6 0.1 convert_element_type.44
  151.7 0.6 copy.32
  152.4 5.1 %all-to-all-start.1 = ((bf16[4,4,96,16]{2,3,1,0:T(8,128)(2,1)}), bf16[4,4,96,16]{2,3,1,0:T(8,128)(2,1)S(1)}, u32[]{:S(2)}, u32[]{:S(2)}) async-start(bf16[4,4,96,16]{2,3,1,0:T(8,128)(2,1)} %copy.32), calls=%async_computation.1 | async-start | bytes 131072 | tf_op jit(solution)/shard_map/all_to_all | solution.py:102
  157.5 3.4 %fusion.11 = bf16[4,16,1280]{2,1,0:T(8,128)(2,1)} fusion(bf16[4,4,96,1280]{3,2,1,0:T(8,128)(2,1)} %all-to-all-done.2, f32[4]{0:T(128)S(1)} %broadcast_divide_fusion, bf16[4,16,4,96]{3,2,1,0:T(4,128)(2,1)S(1)} %convert_element_type.37), kind=kOutput, calls=%fused_computation.13 | convolution fusion | flops 63078400 | bytes 4145168 | tf_op jit(solution)/shard_map/arnc,nacd->ard/dot_general | solution.py:90
  160.9 0.8 fusion.20
  161.8 1.4 all-to-all-done.1
  163.2 3.1 %convolution_convert_fusion = bf16[16,96,1280]{2,1,0:T(8,128)(2,1)} fusion(bf16[16,96,16]{1,2,0:T(8,128)(2,1)S(1)} %bitcast.58, bf16[16,16,1280]{2,1,0:T(8,128)(2,1)S(1)} %all_gather.7), kind=kOutput, calls=%fused_computation.4 | convolution fusion | flops 64880640 | bytes 4636672 | tf_op jit(solution)/shard_map/acr,ard->acd/dot_general | solution.py:106
  166.3 5.7 %gather_fusion = bf16[512,1280]{1,0:T(8,128)(2,1)S(1)} fusion(bf16[1536,1280]{1,0:T(8,128)(2,1)} %bitcast.56, s32[1024]{0:T(1024)S(1)} %pad_clamp_fusion), kind=kCustom, calls=%fused_computation | custom fusion | bytes 2623488 | tf_op jit(solution)/shard_map/gather | solution.py:115
  172.1 0.0 copy-done
  172.1 2.0 %fusion.4 = bf16[512,1280]{1,0:T(8,128)(2,1)} fusion(bf16[512,512]{1,0:T(8,128)(2,1)S(1)} %all_gather.6, bf16[1280,512]{1,0:T(8,128)(2,1)S(1)} %copy-done, bf16[512,1280]{1,0:T(8,128)(2,1)S(1)} %gather_fusion), kind=kOutput, calls=%fused_computation.10 | convolution fusion | flops 673710080 | bytes 4456448 | tf_op jit(solution)/shard_map/dot_general | solution.py:26
  (8 shorter events, 0.1 us)
Async XLA Ops:
  0.6 171.4 %copy-start = (bf16[1280,512]{1,0:T(8,128)(2,1)S(1)}, bf16[1280,512]{1,0:T(8,128)(2,1)}, u32[]{:S(2)}) copy-start(bf16[1280,512]{1,0:T(8,128)(2,1)} %param.9) | copy-start | bytes 3932164
  7.6 11.9 %all-to-all-start.3 = ((bf16[4,4,96]{2,1,0:T(4,128)(2,1)}), bf16[4,4,96]{2,1,0:T(4,128)(2,1)S(1)}, u32[]{:S(2)}, u32[]{:S(2)}) async-start(bf16[4,4,96]{2,1,0:T(4,128)(2,1)} %reshape.88), calls=%async_computation.3 | async-start | bytes 8192 | tf_op jit(solution)/shard_map/all_to_all | solution.py:67
  19.4 14.0 %all-to-all-start = ((bf16[4,4,96,128]{3,2,1,0:T(8,128)(2,1)}), bf16[4,4,96,128]{3,2,1,0:T(8,128)(2,1)S(1)}, u32[]{:S(2)}, u32[]{:S(2)}) async-start(bf16[4,4,96,128]{3,2,1,0:T(8,128)(2,1)} %bitcast.5), calls=%async_computation | async-start | bytes 786432 | tf_op jit(solution)/shard_map/all_to_all | solution.py:60
  33.4 5.0 %copy-start.2 = (bf16[512,128]{1,0:T(8,128)(2,1)S(1)}, bf16[512,128]{1,0:T(8,128)(2,1)}, u32[]{:S(2)}) copy-start(bf16[512,128]{1,0:T(8,128)(2,1)} %param.8) | copy-start | bytes 393220
  33.4 12.2 %copy-start.1 = (bf16[4,16,1280]{2,1,0:T(8,128)(2,1)S(1)}, bf16[4,16,1280]{2,1,0:T(8,128)(2,1)}, u32[]{:S(2)}) copy-start(bf16[4,16,1280]{2,1,0:T(8,128)(2,1)} %param.10) | copy-start | bytes 491524
  33.4 101.8 %copy-start.3 = (bf16[4,16,128]{2,1,0:T(8,128)(2,1)S(1)}, bf16[4,16,128]{2,1,0:T(8,128)(2,1)}, u32[]{:S(2)}) copy-start(bf16[4,16,128]{2,1,0:T(8,128)(2,1)} %param.11) | copy-start | bytes 49156
  33.4 102.4 %all-to-all-start.2 = ((bf16[4,4,96,1280]{3,2,1,0:T(8,128)(2,1)}), bf16[4,4,96,1280]{3,2,1,0:T(8,128)(2,1)}, u32[]{:S(2)}, u32[]{:S(2)}) async-start(bf16[4,4,96,1280]{3,2,1,0:T(8,128)(2,1)} %bitcast.57), calls=%async_computation.2 | async-start | bytes 7864320 | tf_op jit(solution)/shard_map/all_to_all | solution.py:53
  152.4 10.8 %all-to-all-start.1 = ((bf16[4,4,96,16]{2,3,1,0:T(8,128)(2,1)}), bf16[4,4,96,16]{2,3,1,0:T(8,128)(2,1)S(1)}, u32[]{:S(2)}, u32[]{:S(2)}) async-start(bf16[4,4,96,16]{2,3,1,0:T(8,128)(2,1)} %copy.32), calls=%async_computation.1 | async-start | bytes 131072 | tf_op jit(solution)/shard_map/all_to_all | solution.py:102
where the time goes:
time: 175 us; the launch traced here: 174 us
  blocking collectives  109 us (62%)
  local copies, waits for them, and re-layouts  20.6 us (12%)
  starting transfers between devices  19.8 us (11%)
  matrix products  13.1 us (7%)
  waiting for transfers between devices  8.56 us (5%)
  other arithmetic  2.32 us (1%)
    all_gather x1, blocking collectives, shards(): lax.all_gather(adapter_lower_factor, 'replica', axis=0, tiled=True)  89.5 us
    psum x1, blocking collectives, shards(): lax.psum((lower_factor_share.reshape(flat_shape), upper_factor_share.resh...  12.2 us
    all_gather x1, blocking collectives, shards(): lax.all_gather(value_output_gradient, 'tensor', axis=1, tiled=True)  7.2 us
    all_to_all x1, starting transfers between devices, shards(): lax.all_to_all(marks_send.reshape(replicas, local_owned_count, capacity),...  6.32 us
    scatter x1, local copies, waits for them, and re-layouts, shards(): rows_send = jnp.zeros((slot_total_count, share_width), jnp.bfloat16).at[d...  6.11 us
    gather x1, local copies, waits for them, and re-layouts, shards(): selected_rows = adapter_token_rows[destination_index]  5.74 us
    all_to_all x1, starting transfers between devices, shards(): lax.all_to_all(coeff_send, 'replica', split_axis=0, concat_axis=0, tiled=...  5.09 us
    all_to_all x1, starting transfers between devices, shards(): lax.all_to_all(rows_send.reshape(replicas, local_owned_count, capacity, s...  4.93 us
  transfers between devices with their start and end apart: 4, of which 3 were waited for; matrix products, arithmetic and copies ran while one was open for 8% of the time, Pallas kernels for 0%

commit v1 on v0

--- a/solution.py
+++ b/solution.py
@@ -1,12 +1,462 @@
+import functools
+import math
+
 import jax
 import jax.numpy as jnp
 from jax import lax
+from jax.experimental import pallas as pl
+from jax.experimental.pallas import tpu as pltpu
 from jax.sharding import PartitionSpec as P
 
 SCALING = 2.0
 
+MESH = pl.DeviceIdType.MESH
+F32 = jnp.float32
+BF16 = jnp.bfloat16
+
+
+def fused_body(
+    replicas,
+    tensors,
+    owned,
+    x_hbm,
+    v_hbm,
+    w_hbm,
+    a_hbm,
+    b_hbm,
+    ids_ref,
+    table_ref,
+    hid_hbm,
+    down_ref,
+    up_ref,
+    x,
+    w,
+    v_own,
+    v_full,
+    a_all,
+    b_all,
+    hid,
+    cu_all,
+    cd_all,
+    cm,
+    cmt,
+    part,
+    snd,
+    hop_r,
+    hop_l,
+    up_part,
+    up_all,
+    cnt_part,
+    cnt_all,
+    load_sem,
+    a_send_r,
+    a_send_l,
+    a_recv,
+    rs_send,
+    rs_recv_r,
+    rs_recv_l,
+    b_send,
+    b_recv,
+    v_send,
+    v_recv,
+    cu_send,
+    cu_recv,
+    cd_send,
+    cd_recv,
+    up_send,
+    up_recv,
+    cnt_send,
+    cnt_recv,
+):
+    R, T = replicas, tensors
+    me = lax.axis_index("replica")
+    mt = lax.axis_index("tensor")
+    rows = a_hbm.shape[0]
+    rank = rows // owned
+    tokens, width = x_hbm.shape
+    vshare = v_hbm.shape[1]
+    adapters = R * owned
+
+    def remote(src, dst, send, recv, axis, to):
+        return pltpu.make_async_remote_copy(
+            src_ref=src, dst_ref=dst, send_sem=send, recv_sem=recv,
+            device_id={axis: to}, device_id_type=MESH,
+        )
+
+    def peers(axis):
+        n, here = (R, me) if axis == "replica" else (T, mt)
+        return [lax.rem(here + d, n) for d in range(1, n)]
+
+    def vcols(i):
+        return v_full.at[:, pl.ds(pl.multiple_of(i * vshare, vshare), vshare)]
+
+    loads = {
+        "b": pltpu.make_async_copy(b_hbm, b_all.at[me], load_sem.at[0]),
+        "v": pltpu.make_async_copy(v_hbm, v_own, load_sem.at[1]),
+        "x": pltpu.make_async_copy(x_hbm, x, load_sem.at[2]),
+        "a": pltpu.make_async_copy(a_hbm, a_all.at[me], load_sem.at[3]),
+        "vf": pltpu.make_async_copy(v_hbm, vcols(mt), load_sem.at[4]),
+        "w": pltpu.make_async_copy(w_hbm, w, load_sem.at[5]),
+    }
+    for name in ("b", "v", "x", "a", "vf", "w"):
+        loads[name].start()
+
+    barrier = pltpu.get_barrier_semaphore()
+    for axis in ("replica", "tensor"):
+        for to in peers(axis):
+            pl.semaphore_signal(barrier, inc=1, device_id={axis: to}, device_id_type=MESH)
+
+    ids = ids_ref[...]
+    slot = jnp.zeros_like(ids)
+    for i in range(adapters):
+        slot = jnp.where(ids == i, table_ref[i], slot)
+    slot = jnp.broadcast_to(slot, (rank, tokens))
+    pad = cnt_part.shape[1]
+    for j in range(R):
+        which = lax.broadcasted_iota(jnp.int32, (pad, tokens), 0)
+        hit = (slot[0:pad, :] == which + j * owned) & (which < owned)
+        total = jnp.sum(hit.astype(F32), axis=1, keepdims=True)
+        cnt_part[j] = jnp.broadcast_to(total, (pad, 128))
+
+    pl.semaphore_wait(barrier, R - 1 + T - 1)
+
+    b_out = [
+        remote(b_hbm, b_all.at[me], b_send.at[d], b_recv.at[me], "replica", to)
+        for d, to in enumerate(peers("replica"))
+    ]
+    for copy in b_out:
+        copy.start()
+
+    def a_right(j, k, src):
+        return remote(src, a_all.at[j], a_send_r.at[k], a_recv.at[j], "replica", me + 1)
+
+    def a_left(j, k, src):
+        return remote(src, a_all.at[j], a_send_l.at[k], a_recv.at[j], "replica", me - 1)
+
+    @pl.when(me < R - 1)
+    def _():
+        a_right(me, 0, a_hbm).start()
+
+    @pl.when(me > 0)
+    def _():
+        a_left(me, 0, a_hbm).start()
+
+    cnt_out = [
+        remote(cnt_part.at[to], cnt_all.at[me], cnt_send.at[d], cnt_recv.at[me], "replica", to)
+        for d, to in enumerate(peers("replica"))
+    ]
+    for copy in cnt_out:
+        copy.start()
+    cnt_all[me] = cnt_part[me]
+
+    loads["b"].wait()
+    loads["v"].wait()
+    for to in peers("replica"):
+        remote(b_hbm, b_all.at[to], b_send.at[0], b_recv.at[to], "replica", to).wait_recv()
+    product = lax.dot_general(
+        b_all[...].reshape(R * rows, vshare), v_own[...], (((1,), (1,)), ((), ())),
+        preferred_element_type=F32,
+    )
+    cu = jnp.zeros((rank, tokens), F32)
+    for s in range(adapters):
+        cu = jnp.where(slot == s, product[s * rank:(s + 1) * rank, :], cu)
+    cu_all[mt] = cu
+    cu_out = [
+        remote(cu_all.at[mt], cu_all.at[mt], cu_send.at[d], cu_recv.at[mt], "tensor", to)
+        for d, to in enumerate(peers("tensor"))
+    ]
+    for copy in cu_out:
+        copy.start()
+    v_out = [
+        remote(v_hbm, vcols(mt), v_send.at[d], v_recv.at[mt], "tensor", to)
+        for d, to in enumerate(peers("tensor"))
+    ]
+    for copy in v_out:
+        copy.start()
+
+    def a_hop(k):
+        @pl.when(me >= k)
+        def _():
+            j = me - k
+            a_right(j, k, a_all.at[j]).wait_recv()
+            if k < R - 1:
+                @pl.when(me < R - 1)
+                def _():
+                    a_right(j, k, a_all.at[j]).start()
+
+        @pl.when(me + k < R)
+        def _():
+            j = me + k
+            a_left(j, k, a_all.at[j]).wait_recv()
+            if k < R - 1:
+                @pl.when(me > 0)
+                def _():
+                    a_left(j, k, a_all.at[j]).start()
+
+    def add_cd(j):
+        p = lax.dot_general(
+            a_all[j], x[...], (((1,), (1,)), ((), ())), preferred_element_type=F32
+        )
+        acc = cd_all[mt]
+        for s in range(owned):
+            acc = jnp.where(slot == j * owned + s, p[s * rank:(s + 1) * rank, :], acc)
+        cd_all[mt] = acc
+
+    def cd_hop(k):
+        @pl.when(me >= k)
+        def _():
+            add_cd(me - k)
+
+        @pl.when(me + k < R)
+        def _():
+            add_cd(me + k)
+
+    loads["a"].wait()
+    loads["x"].wait()
+    a_hop(1)
+
+    for to in peers("tensor"):
+        remote(cu_all.at[to], cu_all.at[to], cu_send.at[0], cu_recv.at[to], "tensor", to).wait_recv()
+    c = cu_all[0]
+    for q in range(1, T):
+        c = c + cu_all[q]
+    c = c.astype(BF16).astype(F32)
+    spread = jnp.concatenate([jnp.where(slot == s, c, 0.0) for s in range(adapters)], axis=0)
+    cm[...] = spread.astype(BF16).reshape(R, rows, tokens)
+
+    def rs_right(d):
+        return remote(snd.at[d], hop_r.at[d], rs_send.at[d], rs_recv_r.at[d], "replica", me + 1)
+
+    def rs_left(d):
+        return remote(snd.at[d], hop_l.at[d], rs_send.at[d], rs_recv_l.at[d], "replica", me - 1)
+
+    order = []
+    for i in range((R + 1) // 2):
+        order += [R - 1 - i] + ([i] if i != R - 1 - i else [])
+    for j in order:
+        p = jnp.dot(cm[j], x[...], preferred_element_type=F32)
+        part[j] = p
+        if j > 0:
+            @pl.when(me == 0)
+            def _():
+                snd[j] = part[j].astype(BF16)
+                rs_right(j).start()
+        if j < R - 1:
+            @pl.when(me == R - 1)
+            def _():
+                snd[j] = part[j].astype(BF16)
+                rs_left(j).start()
+
+    def relay(k):
+        d = R - 1 - k
+
+        @pl.when((me > 0) & (me < d))
+        def _():
+            rs_right(d).wait_recv()
+            snd[d] = (part[d] + hop_r[d].astype(F32)).astype(BF16)
+            rs_right(d).start()
+
+        @pl.when((me < R - 1) & (me > k))
+        def _():
+            rs_left(k).wait_recv()
+            snd[k] = (part[k] + hop_l[k].astype(F32)).astype(BF16)
+            rs_left(k).start()
+
+    cd_all[mt] = jnp.zeros((rank, tokens), F32)
+    add_cd(me)
+    a_hop(2)
+    cd_hop(1)
+    relay(0)
+    cmt[...] = spread.T.astype(BF16)
+    cd_hop(2)
+    for k in range(3, R):
+        a_hop(k)
+        cd_hop(k)
+    cd_out = [
+        remote(cd_all.at[mt], cd_all.at[mt], cd_send.at[d], cd_recv.at[mt], "tensor", to)
+        for d, to in enumerate(peers("tensor"))
+    ]
+    for copy in cd_out:
+        copy.start()
+    for k in range(1, R - 1):
+        relay(k)
+
+    for to in peers("tensor"):
+        remote(cd_all.at[to], cd_all.at[to], cd_send.at[0], cd_recv.at[to], "tensor", to).wait_recv()
+    c = cd_all[0]
+    for q in range(1, T):
+        c = c + cd_all[q]
+    c = c.astype(BF16).astype(F32)
+    spread = jnp.concatenate([jnp.where(slot == s, c, 0.0) for s in range(adapters)], axis=0)
+    up_part[...] = jnp.dot(
+        spread.astype(BF16), v_own[...], preferred_element_type=F32
+    ).reshape(R, rows, vshare)
+    up_out = [
+        remote(up_part.at[to], up_all.at[me], up_send.at[d], up_recv.at[me], "replica", to)
+        for d, to in enumerate(peers("replica"))
+    ]
+    for copy in up_out:
+        copy.start()
+    up_all[me] = up_part[me]
+
+    loads["vf"].wait()
+    loads["w"].wait()
+    for to in peers("tensor"):
+        remote(v_hbm, vcols(to), v_send.at[0], v_recv.at[to], "tensor", to).wait_recv()
+    tile = 256 if width % 256 == 0 else 128
+
+    @pl.loop(0, width // tile)
+    def _(i):
+        at = pl.ds(pl.multiple_of(i * tile, tile), tile)
+        lora = jnp.dot(
+            cmt[...], a_all[:, :, at].reshape(R * rows, tile), preferred_element_type=F32
+        ).astype(BF16).astype(F32)
+        base = lax.dot_general(
+            v_full[...], w[at, :], (((1,), (1,)), ((), ())), preferred_element_type=F32
+        )
+        hid[:, at] = (base + SCALING * lora).astype(BF16)
+
+    hid_out = pltpu.make_async_copy(hid, hid_hbm, load_sem.at[6])
+    hid_out.start()
+
+    for to in peers("replica"):
+        remote(cnt_part.at[to], cnt_all.at[to], cnt_send.at[0], cnt_recv.at[to], "replica", to).wait_recv()
+    count = cnt_all[0]
+    for j in range(1, R):
+        count = count + cnt_all[j]
+    count = jnp.where(lax.broadcasted_iota(jnp.int32, count.shape, 0) < owned, count, 1.0)
+    factor = SCALING / count
+
+    @pl.when(me > 0)
+    def _():
+        rs_right(me).wait_recv()
+        part[me] = part[me] + hop_r[me].astype(F32)
+
+    @pl.when(me < R - 1)
+    def _():
+        rs_left(me).wait_recv()
+        part[me] = part[me] + hop_l[me].astype(F32)
+
+    for s in range(owned):
+        at = pl.ds(s * rank, rank)
+        down_ref[at, :] = (part[me, at, :] * factor[s:s + 1, 0:1]).astype(BF16)
+
+    for to in peers("replica"):
+        remote(up_part.at[to], up_all.at[to], up_send.at[0], up_recv.at[to], "replica", to).wait_recv()
+    total = up_all[0]
+    for j in range(1, R):
+        total = total + up_all[j]
+    for s in range(owned):
+        at = slice(s * rank, (s + 1) * rank)
+        up_ref[at, :] = (total[at, :] * factor[s:s + 1, 0:1]).astype(BF16)
+
+    for copy in b_out + cnt_out + cu_out + v_out + cd_out + up_out:
+        copy.wait_send()
+    for k in range(R - 1):
+        @pl.when((me >= k) & (me < R - 1))
+        def _():
+            a_right(me - k, k, a_all.at[me - k]).wait_send()
+
+        @pl.when((me + k < R) & (me > 0))
+        def _():
+            a_left(me + k, k, a_all.at[me + k]).wait_send()
+    for d in range(R):
+        @pl.when(me < d)
+        def _():
+            rs_right(d).wait_send()
+
+        @pl.when(me > d)
+        def _():
+            rs_left(d).wait_send()
+    hid_out.wait()
+
+
+def scratch_of(R, T, owned, rank, tokens, width, vshare):
+    rows = owned * rank
+    features = T * vshare
+    pad = -(-owned // 8) * 8
+    buffers = [
+        ((tokens, width), BF16),
+        ((width, features), BF16),
+        ((tokens, vshare), BF16),
+        ((tokens, features), BF16),
+        ((R, rows, width), BF16),
+        ((R, rows, vshare), BF16),
+        ((tokens, width), BF16),
+        ((T, rank, tokens), F32),
+        ((T, rank, tokens), F32),
+        ((R, rows, tokens), BF16),
+        ((tokens, R * rows), BF16),
+        ((R, rows, width), F32),
+        ((R, rows, width), BF16),
+        ((R, rows, width), BF16),
+        ((R, rows, width), BF16),
+        ((R, rows, vshare), F32),
+        ((R, rows, vshare), F32),
+        ((R, pad, 128), F32),
+        ((R, pad, 128), F32),
+    ]
+    sems = [7] + [R] * 6 + [R, R, T, T, T, T, T, T, R, R, R, R]
+    size = sum(math.prod(shape) * jnp.dtype(kind).itemsize for shape, kind in buffers)
+    return size, [pltpu.VMEM(*b) for b in buffers] + [pltpu.SemaphoreType.DMA((n,)) for n in sems]
+
+
+VMEM_LIMIT = 40 * 1024 * 1024
+
 
 def shards(
+    hidden_input_saved,
+    value_output_gradient,
+    frozen_value_weight,
+    adapter_lower_factor,
+    adapter_upper_factor,
+    per_token_adapter,
+    adapter_table_slot,
+):
+    R, T = lax.axis_size("replica"), lax.axis_size("tensor")
+    owned, rank, width = adapter_lower_factor.shape
+    vshare = adapter_upper_factor.shape[2]
+    tokens = hidden_input_saved.shape[0]
+    size, scratch = scratch_of(R, T, owned, rank, tokens, width, vshare)
+    if size > VMEM_LIMIT // 2:
+        return dispatched(
+            hidden_input_saved, value_output_gradient, frozen_value_weight,
+            adapter_lower_factor, adapter_upper_factor, per_token_adapter, adapter_table_slot,
+        )
+    rows = owned * rank
+    anywhere = pl.BlockSpec(memory_space=pl.ANY)
+    vmem = pl.BlockSpec(memory_space=pltpu.VMEM)
+    hidden_grad, down_grad, up_grad = pl.pallas_call(
+        functools.partial(fused_body, R, T, owned),
+        out_shape=(
+            jax.ShapeDtypeStruct((tokens, width), BF16),
+            jax.ShapeDtypeStruct((rows, width), BF16),
+            jax.ShapeDtypeStruct((rows, vshare), BF16),
+        ),
+        in_specs=[anywhere] * 5 + [vmem, pl.BlockSpec(memory_space=pltpu.SMEM)],
+        out_specs=(anywhere, vmem, vmem),
+        scratch_shapes=scratch,
+        compiler_params=pltpu.CompilerParams(
+            collective_id=0, has_side_effects=True, vmem_limit_bytes=VMEM_LIMIT
+        ),
+        name="lora_value_backward",
+    )(
+        hidden_input_saved,
+        value_output_gradient,
+        frozen_value_weight,
+        adapter_lower_factor.reshape(rows, width),
+        adapter_upper_factor.reshape(rows, vshare),
+        per_token_adapter.reshape(1, tokens),
+        adapter_table_slot,
+    )
+    return (
+        hidden_grad,
+        down_grad.reshape(owned, rank, width),
+        up_grad.reshape(owned, rank, vshare),
+    )
+
+
+def dispatched(
     hidden_input_saved,
     value_output_gradient,
     frozen_value_weight,

time: 175 us -> 49.9 us (0.29)
  blocking collectives: 109 us -> 0 us
  Pallas kernels: 0 us -> 40.1 us
  starting transfers between devices: 19.8 us -> 0 us
  matrix products: 13.1 us -> 0 us
  local copies, waits for them, and re-layouts: 20.6 us -> 8.83 us
  waiting for transfers between devices: 8.56 us -> 0 us
  other arithmetic: 2.32 us -> 0 us
    all_gather x2 -> x0, blocking collectives: 96.7 us -> none  [the longest x1 89.5 us: shards(): lax.all_gather(adapter_lower_factor, 'replica', axis=0, tiled=True)]
    pallas_call x0 -> x1, Pallas kernels: none -> 40.1 us  [shards(): pl.pallas_call(functools.partial(fused_body, R, T, owned), out_shape=(jax...]
    all_to_all x4 -> x0, starting transfers between devices: 19.8 us -> none  [the longest x1 6.32 us: shards(): lax.all_to_all(marks_send.reshape(replicas, local_owned_count, capacity),...]
    dot_general x6 -> x0, matrix products: 13.1 us -> none  [the longest x1 3.45 us: shards(): jnp.einsum('arnc,nacd->ard', upper_coefficient, incoming_rows, preferred_...]
    scatter x3 -> x0, local copies, waits for them, and re-layouts: 12.7 us -> none  [the longest x1 6.11 us: shards(): rows_send = jnp.zeros((slot_total_count, share_width), jnp.bfloat16).at[d...]
    psum x1 -> x0, blocking collectives: 12.2 us -> none  [shards(): lax.psum((lower_factor_share.reshape(flat_shape), upper_factor_share.resh...]
    unnamed x8 -> x17, local copies, waits for them, and re-layouts: 0.02 us -> 8.83 us
    all_to_all x4 -> x0, waiting for transfers between devices: 8.56 us -> none  [the longest x1 4.39 us: shards(): lax.all_to_all(value_send.reshape(replicas, local_owned_count, capacity,...]
  transfers between devices with their start and end apart: 4 -> 0, of which waited for: 3 -> 0; matrix products, arithmetic and copies ran while one was open for 8% -> 0% of each run, Pallas kernels for 0% -> 0%
where the time goes in v1:
time: 49.9 us; the launch traced here: 49.6 us
  Pallas kernels  40.1 us (80%)
  local copies, waits for them, and re-layouts  8.83 us (18%)
  between operations  0.66 us (1%)
    pallas_call x1, Pallas kernels, shards(): pl.pallas_call(functools.partial(fused_body, R, T, owned), out_shape=(jax...  40.1 us
    unnamed x17, local copies, waits for them, and re-layouts  8.83 us

profile of v1, /device:TPU:0, one launch (start us, length us, event | category | flops | bytes accessed | tf_op | source)
XLA Modules:
  0.0 49.6 jit_solution(239374806656376342)
XLA Ops:
  0.6 0.0 copy-start
  0.6 1.3 %copy-done = bf16[512,1280]{1,0:T(8,128)(2,1)S(1)} copy-done((bf16[512,1280]{1,0:T(8,128)(2,1)S(1)}, bf16[512,1280]{1,0:T(8,128)(2,1)}, u32[]{:S(2)}) %copy-start) | copy-done | bytes 1310744
  1.9 0.0 copy-start.1
  2.0 1.3 %copy-done.1 = bf16[1280,512]{1,0:T(8,128)(2,1)S(1)} copy-done((bf16[1280,512]{1,0:T(8,128)(2,1)S(1)}, bf16[1280,512]{1,0:T(8,128)(2,1)}, u32[]{:S(2)}) %copy-start.1) | copy-done | bytes 1310744
  3.3 0.0 copy-start.2
  3.3 0.9 %copy-done.2 = bf16[4,16,1280]{2,1,0:T(8,128)(2,1)S(1)} copy-done((bf16[4,16,1280]{2,1,0:T(8,128)(2,1)S(1)}, bf16[4,16,1280]{2,1,0:T(8,128)(2,1)}, u32[]{:S(2)}) %copy-start.2) | copy-done | bytes 163864
  4.2 0.0 copy-start.3
  4.2 0.9 %copy-done.3 = bf16[512,128]{1,0:T(8,128)(2,1)S(1)} copy-done((bf16[512,128]{1,0:T(8,128)(2,1)S(1)}, bf16[512,128]{1,0:T(8,128)(2,1)}, u32[]{:S(2)}) %copy-start.3) | copy-done | bytes 131096
  5.1 0.0 copy-start.4
  5.1 0.7 %copy-done.4 = bf16[4,16,128]{2,1,0:T(8,128)(2,1)S(1)} copy-done((bf16[4,16,128]{2,1,0:T(8,128)(2,1)S(1)}, bf16[4,16,128]{2,1,0:T(8,128)(2,1)}, u32[]{:S(2)}) %copy-start.4) | copy-done | bytes 16408
  5.8 0.0 copy-start.5
  5.8 0.7 %copy-done.5 = s32[512,1]{0,1:T(1,128)S(1)} copy-done((s32[512,1]{0,1:T(1,128)S(1)}, s32[512,1]{0,1:T(1,128)}, u32[]{:S(2)}) %copy-start.5) | copy-done | bytes 2072
  6.5 0.0 copy-start.6
  6.5 0.7 %copy-done.6 = s32[16]{0:T(128)S(1)} copy-done((s32[16]{0:T(128)S(1)}, s32[16]{0:T(128)}, u32[]{:S(2)}) %copy-start.6) | copy-done | bytes 88
  7.1 40.1 %lora_value_backward.1 = (bf16[512,1280]{1,0:T(8,128)(2,1)S(1)}, bf16[64,1280]{1,0:T(8,128)(2,1)S(1)}, bf16[64,128]{1,0:T(8,128)(2,1)S(1)}) custom-call(bf16[512,1280]{1,0:T(8,128)(2,1)S(1)} %copy-done, bf16[512,128]{1,0:T(8,128)(2,1)S(1)} %copy-done.3, bf16[1280,512]{1,0:T(8,128)(2,1)S(1)} %copy-done.1, bf16[64,1280]{1,0:T(8,128)(2,1)S(1)} %bitcast.5, ...), custom_call_target="tpu_custom_call" | custom-call | tf_op jit(solution)/shard_map/lora_value_backward/pallas_call | solution.py:429
  47.2 1.1 %copy.13 = bf16[512,1280]{1,0:T(8,128)(2,1)} copy(bf16[512,1280]{1,0:T(8,128)(2,1)S(1)} %get-tuple-element.12) | data formatting | bytes 2621440
  48.3 0.7 %copy.14 = bf16[4,16,1280]{2,1,0:T(8,128)(2,1)} copy(bf16[4,16,1280]{2,1,0:T(8,128)(2,1)S(1)} %bitcast.6) | data formatting | bytes 327680
  49.0 0.6 %copy.15 = bf16[4,16,128]{2,1,0:T(8,128)(2,1)} copy(bf16[4,16,128]{2,1,0:T(8,128)(2,1)S(1)} %bitcast.8) | data formatting | bytes 32768
Async XLA Ops:
  0.6 1.3 %copy-start = (bf16[512,1280]{1,0:T(8,128)(2,1)S(1)}, bf16[512,1280]{1,0:T(8,128)(2,1)}, u32[]{:S(2)}) copy-start(bf16[512,1280]{1,0:T(8,128)(2,1)} %x_hbm.1) | copy-start | bytes 3932164
  1.9 1.3 %copy-start.1 = (bf16[1280,512]{1,0:T(8,128)(2,1)S(1)}, bf16[1280,512]{1,0:T(8,128)(2,1)}, u32[]{:S(2)}) copy-start(bf16[1280,512]{1,0:T(8,128)(2,1)} %w_hbm.1) | copy-start | bytes 3932164
  3.3 0.9 %copy-start.2 = (bf16[4,16,1280]{2,1,0:T(8,128)(2,1)S(1)}, bf16[4,16,1280]{2,1,0:T(8,128)(2,1)}, u32[]{:S(2)}) copy-start(bf16[4,16,1280]{2,1,0:T(8,128)(2,1)} %param.10) | copy-start | bytes 491524
  4.2 0.9 %copy-start.3 = (bf16[512,128]{1,0:T(8,128)(2,1)S(1)}, bf16[512,128]{1,0:T(8,128)(2,1)}, u32[]{:S(2)}) copy-start(bf16[512,128]{1,0:T(8,128)(2,1)} %v_hbm.1) | copy-start | bytes 393220
  5.1 0.7 %copy-start.4 = (bf16[4,16,128]{2,1,0:T(8,128)(2,1)S(1)}, bf16[4,16,128]{2,1,0:T(8,128)(2,1)}, u32[]{:S(2)}) copy-start(bf16[4,16,128]{2,1,0:T(8,128)(2,1)} %param.11) | copy-start | bytes 49156
  5.8 0.7 %copy-start.5 = (s32[512,1]{0,1:T(1,128)S(1)}, s32[512,1]{0,1:T(1,128)}, u32[]{:S(2)}) copy-start(s32[512,1]{0,1:T(1,128)} %param.12) | copy-start | bytes 6148
  6.5 0.7 %copy-start.6 = (s32[16]{0:T(128)S(1)}, s32[16]{0:T(128)}, u32[]{:S(2)}) copy-start(s32[16]{0:T(128)} %table_ref.1) | copy-start | bytes 196

commit v2 on v1

--- a/solution.py
+++ b/solution.py
@@ -24,9 +24,9 @@
     w_hbm,
     a_hbm,
     b_hbm,
-    ids_ref,
-    table_ref,
-    hid_hbm,
+    ids_hbm,
+    table_hbm,
+    hid,
     down_ref,
     up_ref,
     x,
@@ -35,26 +35,25 @@
     v_full,
     a_all,
     b_all,
-    hid,
     cu_all,
     cd_all,
     cm,
     cmt,
     part,
     snd,
-    hop_r,
-    hop_l,
+    hop,
     up_part,
     up_all,
     cnt_part,
     cnt_all,
+    ids_ref,
+    table_ref,
     load_sem,
     a_send_r,
     a_send_l,
     a_recv,
     rs_send,
-    rs_recv_r,
-    rs_recv_l,
+    rs_recv,
     b_send,
     b_recv,
     v_send,
@@ -91,6 +90,8 @@
         return v_full.at[:, pl.ds(pl.multiple_of(i * vshare, vshare), vshare)]
 
     loads = {
+        "ids": pltpu.make_async_copy(ids_hbm, ids_ref, load_sem.at[7]),
+        "table": pltpu.make_async_copy(table_hbm, table_ref, load_sem.at[8]),
         "b": pltpu.make_async_copy(b_hbm, b_all.at[me], load_sem.at[0]),
         "v": pltpu.make_async_copy(v_hbm, v_own, load_sem.at[1]),
         "x": pltpu.make_async_copy(x_hbm, x, load_sem.at[2]),
@@ -98,7 +99,7 @@
         "vf": pltpu.make_async_copy(v_hbm, vcols(mt), load_sem.at[4]),
         "w": pltpu.make_async_copy(w_hbm, w, load_sem.at[5]),
     }
-    for name in ("b", "v", "x", "a", "vf", "w"):
+    for name in ("ids", "table", "b", "v", "x", "a", "vf", "w"):
         loads[name].start()
 
     barrier = pltpu.get_barrier_semaphore()
@@ -106,6 +107,8 @@
         for to in peers(axis):
             pl.semaphore_signal(barrier, inc=1, device_id={axis: to}, device_id_type=MESH)
 
+    loads["ids"].wait()
+    loads["table"].wait()
     ids = ids_ref[...]
     slot = jnp.zeros_like(ids)
     for i in range(adapters):
@@ -224,49 +227,28 @@
     spread = jnp.concatenate([jnp.where(slot == s, c, 0.0) for s in range(adapters)], axis=0)
     cm[...] = spread.astype(BF16).reshape(R, rows, tokens)
 
-    def rs_right(d):
-        return remote(snd.at[d], hop_r.at[d], rs_send.at[d], rs_recv_r.at[d], "replica", me + 1)
-
-    def rs_left(d):
-        return remote(snd.at[d], hop_l.at[d], rs_send.at[d], rs_recv_l.at[d], "replica", me - 1)
+    def rs_to(d):
+        return remote(snd.at[d], hop.at[me], rs_send.at[d], rs_recv.at[me], "replica", d)
 
     order = []
     for i in range((R + 1) // 2):
         order += [R - 1 - i] + ([i] if i != R - 1 - i else [])
     for j in order:
         p = jnp.dot(cm[j], x[...], preferred_element_type=F32)
-        part[j] = p
-        if j > 0:
-            @pl.when(me == 0)
-            def _():
-                snd[j] = part[j].astype(BF16)
-                rs_right(j).start()
-        if j < R - 1:
-            @pl.when(me == R - 1)
-            def _():
-                snd[j] = part[j].astype(BF16)
-                rs_left(j).start()
-
-    def relay(k):
-        d = R - 1 - k
-
-        @pl.when((me > 0) & (me < d))
-        def _():
-            rs_right(d).wait_recv()
-            snd[d] = (part[d] + hop_r[d].astype(F32)).astype(BF16)
-            rs_right(d).start()
-
-        @pl.when((me < R - 1) & (me > k))
-        def _():
-            rs_left(k).wait_recv()
-            snd[k] = (part[k] + hop_l[k].astype(F32)).astype(BF16)
-            rs_left(k).start()
+
+        @pl.when(me == j)
+        def _():
+            part[...] = p
+
+        @pl.when(me != j)
+        def _():
+            snd[j] = p.astype(BF16)
+            rs_to(j).start()
 
     cd_all[mt] = jnp.zeros((rank, tokens), F32)
     add_cd(me)
     a_hop(2)
     cd_hop(1)
-    relay(0)
     cmt[...] = spread.T.astype(BF16)
     cd_hop(2)
     for k in range(3, R):
@@ -278,8 +260,6 @@
     ]
     for copy in cd_out:
         copy.start()
-    for k in range(1, R - 1):
-        relay(k)
 
     for to in peers("tensor"):
         remote(cd_all.at[to], cd_all.at[to], cd_send.at[0], cd_recv.at[to], "tensor", to).wait_recv()
@@ -316,9 +296,6 @@
         )
         hid[:, at] = (base + SCALING * lora).astype(BF16)
 
-    hid_out = pltpu.make_async_copy(hid, hid_hbm, load_sem.at[6])
-    hid_out.start()
-
     for to in peers("replica"):
         remote(cnt_part.at[to], cnt_all.at[to], cnt_send.at[0], cnt_recv.at[to], "replica", to).wait_recv()
     count = cnt_all[0]
@@ -327,19 +304,13 @@
     count = jnp.where(lax.broadcasted_iota(jnp.int32, count.shape, 0) < owned, count, 1.0)
     factor = SCALING / count
 
-    @pl.when(me > 0)
-    def _():
-        rs_right(me).wait_recv()
-        part[me] = part[me] + hop_r[me].astype(F32)
-
-    @pl.when(me < R - 1)
-    def _():
-        rs_left(me).wait_recv()
-        part[me] = part[me] + hop_l[me].astype(F32)
+    for to in peers("replica"):
+        remote(snd.at[to], hop.at[to], rs_send.at[0], rs_recv.at[to], "replica", to).wait_recv()
+        part[...] = part[...] + hop[to].astype(F32)
 
     for s in range(owned):
         at = pl.ds(s * rank, rank)
-        down_ref[at, :] = (part[me, at, :] * factor[s:s + 1, 0:1]).astype(BF16)
+        down_ref[at, :] = (part[at, :] * factor[s:s + 1, 0:1]).astype(BF16)
 
     for to in peers("replica"):
         remote(up_part.at[to], up_all.at[to], up_send.at[0], up_recv.at[to], "replica", to).wait_recv()
@@ -361,14 +332,9 @@
         def _():
             a_left(me + k, k, a_all.at[me + k]).wait_send()
     for d in range(R):
-        @pl.when(me < d)
-        def _():
-            rs_right(d).wait_send()
-
-        @pl.when(me > d)
-        def _():
-            rs_left(d).wait_send()
-    hid_out.wait()
+        @pl.when(me != d)
+        def _():
+            rs_to(d).wait_send()
 
 
 def scratch_of(R, T, owned, rank, tokens, width, vshare):
@@ -382,13 +348,11 @@
         ((tokens, features), BF16),
         ((R, rows, width), BF16),
         ((R, rows, vshare), BF16),
-        ((tokens, width), BF16),
         ((T, rank, tokens), F32),
         ((T, rank, tokens), F32),
         ((R, rows, tokens), BF16),
         ((tokens, R * rows), BF16),
-        ((R, rows, width), F32),
-        ((R, rows, width), BF16),
+        ((rows, width), F32),
         ((R, rows, width), BF16),
         ((R, rows, width), BF16),
         ((R, rows, vshare), F32),
@@ -396,12 +360,13 @@
         ((R, pad, 128), F32),
         ((R, pad, 128), F32),
     ]
-    sems = [7] + [R] * 6 + [R, R, T, T, T, T, T, T, R, R, R, R]
+    sems = [9] + [R] * 5 + [R, R, T, T, T, T, T, T, R, R, R, R]
     size = sum(math.prod(shape) * jnp.dtype(kind).itemsize for shape, kind in buffers)
-    return size, [pltpu.VMEM(*b) for b in buffers] + [pltpu.SemaphoreType.DMA((n,)) for n in sems]
-
-
-VMEM_LIMIT = 40 * 1024 * 1024
+    small = [pltpu.VMEM((1, tokens), jnp.int32), pltpu.SMEM((R * owned,), jnp.int32)]
+    return size, [pltpu.VMEM(*b) for b in buffers] + small + [pltpu.SemaphoreType.DMA((n,)) for n in sems]
+
+
+VMEM_LIMIT = 60 * 1024 * 1024
 
 
 def shards(
@@ -418,7 +383,7 @@
     vshare = adapter_upper_factor.shape[2]
     tokens = hidden_input_saved.shape[0]
     size, scratch = scratch_of(R, T, owned, rank, tokens, width, vshare)
-    if size > VMEM_LIMIT // 2:
+    if size > VMEM_LIMIT // 3:
         return dispatched(
             hidden_input_saved, value_output_gradient, frozen_value_weight,
             adapter_lower_factor, adapter_upper_factor, per_token_adapter, adapter_table_slot,
@@ -429,12 +394,12 @@
     hidden_grad, down_grad, up_grad = pl.pallas_call(
         functools.partial(fused_body, R, T, owned),
         out_shape=(
-            jax.ShapeDtypeStruct((tokens, width), BF16),
+            pltpu.VMEM((tokens, width), BF16),
             jax.ShapeDtypeStruct((rows, width), BF16),
             jax.ShapeDtypeStruct((rows, vshare), BF16),
         ),
-        in_specs=[anywhere] * 5 + [vmem, pl.BlockSpec(memory_space=pltpu.SMEM)],
-        out_specs=(anywhere, vmem, vmem),
+        in_specs=[pl.BlockSpec(memory_space=pltpu.HBM)] * 7,
+        out_specs=(vmem, vmem, vmem),
         scratch_shapes=scratch,
         compiler_params=pltpu.CompilerParams(
             collective_id=0, has_side_effects=True, vmem_limit_bytes=VMEM_LIMIT

time: 49.9 us -> 42.7 us (0.86)
  local copies, waits for them, and re-layouts: 8.83 us -> 2.34 us
  Pallas kernels: 40.1 us -> 39.5 us
    unnamed x17 -> x7, local copies, waits for them, and re-layouts: 8.83 us -> 2.34 us
    pallas_call x1, Pallas kernels: 40.1 us -> 39.5 us  [shards(): pl.pallas_call(functools.partial(fused_body, R, T, owned), out_shape=(plt...]
where the time goes in v2:
time: 42.7 us; the launch traced here: 42.5 us
  Pallas kernels  39.5 us (93%)
  local copies, waits for them, and re-layouts  2.34 us (5%)
  between operations  0.66 us (2%)
    pallas_call x1, Pallas kernels, shards(): pl.pallas_call(functools.partial(fused_body, R, T, owned), out_shape=(plt...  39.5 us
    unnamed x7, local copies, waits for them, and re-layouts  2.34 us

profile of v2, /device:TPU:0, one launch (start us, length us, event | category | flops | bytes accessed | tf_op | source)
XLA Modules:
  0.0 42.5 jit_solution(6223215736499359633)
XLA Ops:
  0.6 39.5 %lora_value_backward.1 = (bf16[512,1280]{1,0:T(8,128)(2,1)S(1)}, bf16[64,1280]{1,0:T(8,128)(2,1)}, bf16[64,128]{1,0:T(8,128)(2,1)}) custom-call(bf16[512,1280]{1,0:T(8,128)(2,1)} %x_hbm.1, bf16[512,128]{1,0:T(8,128)(2,1)} %v_hbm.1, bf16[1280,512]{1,0:T(8,128)(2,1)} %w_hbm.1, bf16[64,1280]{1,0:T(8,128)(2,1)} %bitcast.5, bf16[64,128]{1,0:T(8,128)(2,1)} %bitcast.7, ...), custom_call_target="tpu_custom_call" | custom-call | tf_op jit(solution)/shard_map/lora_value_backward/pallas_call | solution.py:394
  40.2 0.0 copy-start
  40.2 0.0 copy-start.1
  40.2 1.1 %copy.13 = bf16[512,1280]{1,0:T(8,128)(2,1)} copy(bf16[512,1280]{1,0:T(8,128)(2,1)S(1)} %get-tuple-element.9) | data formatting | bytes 2621440
  41.3 0.0 copy-done
  41.3 0.7 %copy.14 = bf16[4,16,1280]{2,1,0:T(8,128)(2,1)} copy(bf16[4,16,1280]{2,1,0:T(8,128)(2,1)S(1)} %bitcast.6) | data formatting | bytes 327680
  41.9 0.0 copy-done.1
  41.9 0.6 %copy.15 = bf16[4,16,128]{2,1,0:T(8,128)(2,1)} copy(bf16[4,16,128]{2,1,0:T(8,128)(2,1)S(1)} %bitcast.8) | data formatting | bytes 32768
Async XLA Ops:
  40.2 1.1 %copy-start = (bf16[64,1280]{1,0:T(8,128)(2,1)S(1)}, bf16[64,1280]{1,0:T(8,128)(2,1)}, u32[]{:S(2)}) copy-start(bf16[64,1280]{1,0:T(8,128)(2,1)} %get-tuple-element.7) | copy-start | bytes 491524
  40.2 1.7 %copy-start.1 = (bf16[64,128]{1,0:T(8,128)(2,1)S(1)}, bf16[64,128]{1,0:T(8,128)(2,1)}, u32[]{:S(2)}) copy-start(bf16[64,128]{1,0:T(8,128)(2,1)} %get-tuple-element.8) | copy-start | bytes 49156

commit v3 on v2

--- a/solution.py
+++ b/solution.py
@@ -42,6 +42,8 @@
     part,
     snd,
     hop,
+    hold,
+    edge,
     up_part,
     up_all,
     cnt_part,
@@ -54,6 +56,7 @@
     a_recv,
     rs_send,
     rs_recv,
+    edge_recv,
     b_send,
     b_recv,
     v_send,
@@ -230,25 +233,57 @@
     def rs_to(d):
         return remote(snd.at[d], hop.at[me], rs_send.at[d], rs_recv.at[me], "replica", d)
 
+    def to_next(d, to):
+        return remote(snd.at[d], edge.at[d], rs_send.at[d], edge_recv.at[d], "replica", to)
+
     order = []
     for i in range((R + 1) // 2):
         order += [R - 1 - i] + ([i] if i != R - 1 - i else [])
     for j in order:
         p = jnp.dot(cm[j], x[...], preferred_element_type=F32)
 
+        from_end = ((me == 1) & (j >= 2)) | ((me == R - 2) & (j <= R - 3))
+        at_start = (me == 0) & (j >= 2)
+        at_stop = (me == R - 1) & (j <= R - 3)
+
         @pl.when(me == j)
         def _():
             part[...] = p
 
-        @pl.when(me != j)
+        @pl.when(from_end)
+        def _():
+            hold[j] = p
+
+        @pl.when((me != j) & jnp.logical_not(from_end))
         def _():
             snd[j] = p.astype(BF16)
+
+        @pl.when(at_start)
+        def _():
+            to_next(j, me + 1).start()
+
+        @pl.when(at_stop)
+        def _():
+            to_next(j, me - 1).start()
+
+        @pl.when((me != j) & jnp.logical_not(from_end | at_start | at_stop))
+        def _():
             rs_to(j).start()
+
+    def pass_on(k):
+        for mine, j in (((me == 1), R - 1 - k), ((me == R - 2), k)):
+            @pl.when(mine)
+            def _():
+                to_next(j, me).wait_recv()
+                snd[j] = (hold[j] + edge[j].astype(F32)).astype(BF16)
+                rs_to(j).start()
 
     cd_all[mt] = jnp.zeros((rank, tokens), F32)
     add_cd(me)
     a_hop(2)
     cd_hop(1)
+    if R > 2:
+        pass_on(0)
     cmt[...] = spread.T.astype(BF16)
     cd_hop(2)
     for k in range(3, R):
@@ -260,6 +295,9 @@
     ]
     for copy in cd_out:
         copy.start()
+
+    for k in range(1, R - 2):
+        pass_on(k)
 
     for to in peers("tensor"):
         remote(cd_all.at[to], cd_all.at[to], cd_send.at[0], cd_recv.at[to], "tensor", to).wait_recv()
@@ -304,9 +342,13 @@
     count = jnp.where(lax.broadcasted_iota(jnp.int32, count.shape, 0) < owned, count, 1.0)
     factor = SCALING / count
 
-    for to in peers("replica"):
-        remote(snd.at[to], hop.at[to], rs_send.at[0], rs_recv.at[to], "replica", to).wait_recv()
-        part[...] = part[...] + hop[to].astype(F32)
+    for j in range(R):
+        passed = ((me >= 2) & (j == 0)) | ((me <= R - 3) & (j == R - 1))
+
+        @pl.when((me != j) & jnp.logical_not(passed))
+        def _():
+            remote(snd.at[j], hop.at[j], rs_send.at[0], rs_recv.at[j], "replica", j).wait_recv()
+            part[...] = part[...] + hop[j].astype(F32)
 
     for s in range(owned):
         at = pl.ds(s * rank, rank)
@@ -355,12 +397,14 @@
         ((rows, width), F32),
         ((R, rows, width), BF16),
         ((R, rows, width), BF16),
+        ((R, rows, width), F32),
+        ((R, rows, width), BF16),
         ((R, rows, vshare), F32),
         ((R, rows, vshare), F32),
         ((R, pad, 128), F32),
         ((R, pad, 128), F32),
     ]
-    sems = [9] + [R] * 5 + [R, R, T, T, T, T, T, T, R, R, R, R]
+    sems = [9] + [R] * 6 + [R, R, T, T, T, T, T, T, R, R, R, R]
     size = sum(math.prod(shape) * jnp.dtype(kind).itemsize for shape, kind in buffers)
     small = [pltpu.VMEM((1, tokens), jnp.int32), pltpu.SMEM((R * owned,), jnp.int32)]
     return size, [pltpu.VMEM(*b) for b in buffers] + small + [pltpu.SemaphoreType.DMA((n,)) for n in sems]

time: 42.7 us -> 40.7 us (0.953)
  Pallas kernels: 39.5 us -> 37.6 us
    pallas_call x1, Pallas kernels: 39.5 us -> 37.6 us  [shards(): pl.pallas_call(functools.partial(fused_body, R, T, owned), out_shape=(plt...]
where the time goes in v3:
time: 40.7 us; the launch traced here: 40.6 us
  Pallas kernels  37.6 us (92%)
  local copies, waits for them, and re-layouts  2.34 us (6%)
  between operations  0.66 us (2%)
    pallas_call x1, Pallas kernels, shards(): pl.pallas_call(functools.partial(fused_body, R, T, owned), out_shape=(plt...  37.6 us
    unnamed x7, local copies, waits for them, and re-layouts  2.34 us

profile of v3, /device:TPU:0, one launch (start us, length us, event | category | flops | bytes accessed | tf_op | source)
XLA Modules:
  0.0 40.6 jit_solution(16720709815534963108)
XLA Ops:
  0.6 37.6 %lora_value_backward.1 = (bf16[512,1280]{1,0:T(8,128)(2,1)S(1)}, bf16[64,1280]{1,0:T(8,128)(2,1)}, bf16[64,128]{1,0:T(8,128)(2,1)}) custom-call(bf16[512,1280]{1,0:T(8,128)(2,1)} %x_hbm.1, bf16[512,128]{1,0:T(8,128)(2,1)} %v_hbm.1, bf16[1280,512]{1,0:T(8,128)(2,1)} %w_hbm.1, bf16[64,1280]{1,0:T(8,128)(2,1)} %bitcast.5, bf16[64,128]{1,0:T(8,128)(2,1)} %bitcast.7, ...), custom_call_target="tpu_custom_call" | custom-call | tf_op jit(solution)/shard_map/lora_value_backward/pallas_call | solution.py:438
  38.2 0.0 copy-start
  38.2 0.0 copy-start.1
  38.2 1.1 %copy.13 = bf16[512,1280]{1,0:T(8,128)(2,1)} copy(bf16[512,1280]{1,0:T(8,128)(2,1)S(1)} %get-tuple-element.9) | data formatting | bytes 2621440
  39.3 0.0 copy-done
  39.3 0.7 %copy.14 = bf16[4,16,1280]{2,1,0:T(8,128)(2,1)} copy(bf16[4,16,1280]{2,1,0:T(8,128)(2,1)S(1)} %bitcast.6) | data formatting | bytes 327680
  40.0 0.0 copy-done.1
  40.0 0.6 %copy.15 = bf16[4,16,128]{2,1,0:T(8,128)(2,1)} copy(bf16[4,16,128]{2,1,0:T(8,128)(2,1)S(1)} %bitcast.8) | data formatting | bytes 32768
Async XLA Ops:
  38.2 1.1 %copy-start = (bf16[64,1280]{1,0:T(8,128)(2,1)S(1)}, bf16[64,1280]{1,0:T(8,128)(2,1)}, u32[]{:S(2)}) copy-start(bf16[64,1280]{1,0:T(8,128)(2,1)} %get-tuple-element.7) | copy-start | bytes 491524
  38.2 1.7 %copy-start.1 = (bf16[64,128]{1,0:T(8,128)(2,1)S(1)}, bf16[64,128]{1,0:T(8,128)(2,1)}, u32[]{:S(2)}) copy-start(bf16[64,128]{1,0:T(8,128)(2,1)} %get-tuple-element.8) | copy-start | bytes 49156

commit v4 on v3

--- a/solution.py
+++ b/solution.py
@@ -177,8 +177,6 @@
         remote(v_hbm, vcols(mt), v_send.at[d], v_recv.at[mt], "tensor", to)
         for d, to in enumerate(peers("tensor"))
     ]
-    for copy in v_out:
-        copy.start()
 
     def a_hop(k):
         @pl.when(me >= k)
@@ -278,6 +276,8 @@
                 snd[j] = (hold[j] + edge[j].astype(F32)).astype(BF16)
                 rs_to(j).start()
 
+    for copy in v_out:
+        copy.start()
     cd_all[mt] = jnp.zeros((rank, tokens), F32)
     add_cd(me)
     a_hop(2)

time: 40.7 us -> 39 us (0.958)
  Pallas kernels: 37.6 us -> 35.9 us
    pallas_call x1, Pallas kernels: 37.6 us -> 35.9 us  [shards(): pl.pallas_call(functools.partial(fused_body, R, T, owned), out_shape=(plt...]
where the time goes in v4:
time: 39 us; the launch traced here: 38.9 us
  Pallas kernels  35.9 us (92%)
  local copies, waits for them, and re-layouts  2.34 us (6%)
  between operations  0.66 us (2%)
    pallas_call x1, Pallas kernels, shards(): pl.pallas_call(functools.partial(fused_body, R, T, owned), out_shape=(plt...  35.9 us
    unnamed x7, local copies, waits for them, and re-layouts  2.34 us

profile of v4, /device:TPU:0, one launch (start us, length us, event | category | flops | bytes accessed | tf_op | source)
XLA Modules:
  0.0 38.9 jit_solution(5952997519148511337)
XLA Ops:
  0.6 35.9 %lora_value_backward.1 = (bf16[512,1280]{1,0:T(8,128)(2,1)S(1)}, bf16[64,1280]{1,0:T(8,128)(2,1)}, bf16[64,128]{1,0:T(8,128)(2,1)}) custom-call(bf16[512,1280]{1,0:T(8,128)(2,1)} %x_hbm.1, bf16[512,128]{1,0:T(8,128)(2,1)} %v_hbm.1, bf16[1280,512]{1,0:T(8,128)(2,1)} %w_hbm.1, bf16[64,1280]{1,0:T(8,128)(2,1)} %bitcast.5, bf16[64,128]{1,0:T(8,128)(2,1)} %bitcast.7, ...), custom_call_target="tpu_custom_call" | custom-call | tf_op jit(solution)/shard_map/lora_value_backward/pallas_call | solution.py:438
  36.5 0.0 copy-start
  36.5 0.0 copy-start.1
  36.5 1.1 %copy.13 = bf16[512,1280]{1,0:T(8,128)(2,1)} copy(bf16[512,1280]{1,0:T(8,128)(2,1)S(1)} %get-tuple-element.9) | data formatting | bytes 2621440
  37.6 0.0 copy-done
  37.6 0.7 %copy.14 = bf16[4,16,1280]{2,1,0:T(8,128)(2,1)} copy(bf16[4,16,1280]{2,1,0:T(8,128)(2,1)S(1)} %bitcast.6) | data formatting | bytes 327680
  38.3 0.0 copy-done.1
  38.3 0.6 %copy.15 = bf16[4,16,128]{2,1,0:T(8,128)(2,1)} copy(bf16[4,16,128]{2,1,0:T(8,128)(2,1)S(1)} %bitcast.8) | data formatting | bytes 32768
Async XLA Ops:
  36.5 1.1 %copy-start = (bf16[64,1280]{1,0:T(8,128)(2,1)S(1)}, bf16[64,1280]{1,0:T(8,128)(2,1)}, u32[]{:S(2)}) copy-start(bf16[64,1280]{1,0:T(8,128)(2,1)} %get-tuple-element.7) | copy-start | bytes 491524
  36.5 1.7 %copy-start.1 = (bf16[64,128]{1,0:T(8,128)(2,1)S(1)}, bf16[64,128]{1,0:T(8,128)(2,1)}, u32[]{:S(2)}) copy-start(bf16[64,128]{1,0:T(8,128)(2,1)} %get-tuple-element.8) | copy-start | bytes 49156

commit v5 on v4

--- a/solution.py
+++ b/solution.py
@@ -308,7 +308,7 @@
     spread = jnp.concatenate([jnp.where(slot == s, c, 0.0) for s in range(adapters)], axis=0)
     up_part[...] = jnp.dot(
         spread.astype(BF16), v_own[...], preferred_element_type=F32
-    ).reshape(R, rows, vshare)
+    ).astype(BF16).reshape(R, rows, vshare)
     up_out = [
         remote(up_part.at[to], up_all.at[me], up_send.at[d], up_recv.at[me], "replica", to)
         for d, to in enumerate(peers("replica"))
@@ -356,9 +356,9 @@
 
     for to in peers("replica"):
         remote(up_part.at[to], up_all.at[to], up_send.at[0], up_recv.at[to], "replica", to).wait_recv()
-    total = up_all[0]
+    total = up_all[0].astype(F32)
     for j in range(1, R):
-        total = total + up_all[j]
+        total = total + up_all[j].astype(F32)
     for s in range(owned):
         at = slice(s * rank, (s + 1) * rank)
         up_ref[at, :] = (total[at, :] * factor[s:s + 1, 0:1]).astype(BF16)
@@ -399,8 +399,8 @@
         ((R, rows, width), BF16),
         ((R, rows, width), F32),
         ((R, rows, width), BF16),
-        ((R, rows, vshare), F32),
-        ((R, rows, vshare), F32),
+        ((R, rows, vshare), BF16),
+        ((R, rows, vshare), BF16),
         ((R, pad, 128), F32),
         ((R, pad, 128), F32),
     ]

time: 39 us -> 38.7 us (level)
  no operation moved by 1% of the time
where the time goes in v5:
time: 38.7 us; the launch traced here: 38.6 us
  Pallas kernels  35.6 us (92%)
  local copies, waits for them, and re-layouts  2.34 us (6%)
  between operations  0.66 us (2%)
    pallas_call x1, Pallas kernels, shards(): pl.pallas_call(functools.partial(fused_body, R, T, owned), out_shape=(plt...  35.6 us
    unnamed x7, local copies, waits for them, and re-layouts  2.34 us

profile of v5, /device:TPU:0, one launch (start us, length us, event | category | flops | bytes accessed | tf_op | source)
XLA Modules:
  0.0 38.6 jit_solution(6049577220244838671)
XLA Ops:
  0.6 35.6 %lora_value_backward.1 = (bf16[512,1280]{1,0:T(8,128)(2,1)S(1)}, bf16[64,1280]{1,0:T(8,128)(2,1)}, bf16[64,128]{1,0:T(8,128)(2,1)}) custom-call(bf16[512,1280]{1,0:T(8,128)(2,1)} %x_hbm.1, bf16[512,128]{1,0:T(8,128)(2,1)} %v_hbm.1, bf16[1280,512]{1,0:T(8,128)(2,1)} %w_hbm.1, bf16[64,1280]{1,0:T(8,128)(2,1)} %bitcast.5, bf16[64,128]{1,0:T(8,128)(2,1)} %bitcast.7, ...), custom_call_target="tpu_custom_call" | custom-call | tf_op jit(solution)/shard_map/lora_value_backward/pallas_call | solution.py:438
  36.2 0.0 copy-start
  36.2 0.0 copy-start.1
  36.2 1.1 %copy.13 = bf16[512,1280]{1,0:T(8,128)(2,1)} copy(bf16[512,1280]{1,0:T(8,128)(2,1)S(1)} %get-tuple-element.9) | data formatting | bytes 2621440
  37.3 0.0 copy-done
  37.3 0.7 %copy.14 = bf16[4,16,1280]{2,1,0:T(8,128)(2,1)} copy(bf16[4,16,1280]{2,1,0:T(8,128)(2,1)S(1)} %bitcast.6) | data formatting | bytes 327680
  38.0 0.0 copy-done.1
  38.0 0.6 %copy.15 = bf16[4,16,128]{2,1,0:T(8,128)(2,1)} copy(bf16[4,16,128]{2,1,0:T(8,128)(2,1)S(1)} %bitcast.8) | data formatting | bytes 32768
Async XLA Ops:
  36.2 1.1 %copy-start = (bf16[64,1280]{1,0:T(8,128)(2,1)S(1)}, bf16[64,1280]{1,0:T(8,128)(2,1)}, u32[]{:S(2)}) copy-start(bf16[64,1280]{1,0:T(8,128)(2,1)} %get-tuple-element.7) | copy-start | bytes 491524
  36.2 1.7 %copy-start.1 = (bf16[64,128]{1,0:T(8,128)(2,1)S(1)}, bf16[64,128]{1,0:T(8,128)(2,1)}, u32[]{:S(2)}) copy-start(bf16[64,128]{1,0:T(8,128)(2,1)} %get-tuple-element.8) | copy-start | bytes 49156
